TPU v7x, 256 devices: a whole 4x4x8 slice. The times are simulated.
256 devices in a mesh: ka: 8 (over x, y_hi), sa: 32 (over y_lo, z, core).
Axes of the slice: x: 4, y: 4 (y_hi: 2, y_lo: 2; y = y_hi * 2 + y_lo), z: 8, core: 2. Of those that a mesh axis runs over, the one named last changes fastest.
Arguments:
- wave_in: float32 [8, 2, 384, 18432], P('ka', None, 'sa'), may hold values from -6 to 6
- potential: float32 [384, 18432], P('sa'), may hold values from -3.140625 to 3.140625
- absorb_radial: float32 [384], P('sa'), may hold values from 0 to 0.6
- absorb_bond: float32 [192], replicated, may hold values from 0 to 0.6
- coriolis_weight: float32 [384], P('sa'), may hold values from 0.002 to 0.03
- ladder: float32 [96, 96], replicated, may hold values from -0.625 to 0.625
- angle_step: float32 [8, 2, 96, 96], P('ka'), may hold values from -0.3125 to 0.3125
- bond_step: float32 [2, 192, 192], replicated, may hold values from -0.21875 to 0.21875
- radial_step: float32 [2, 384, 384], replicated, may hold values from -0.15625 to 0.15625
Outputs:
- wave_out: float32 [8, 2, 384, 18432], P('ka', None, 'sa')
All inputs are finite; a program needn't handle non-finite values.
Results may differ from a plain program's by a relative error of at most 0.00007.
Values sent between devices are 32-bit elements; how exact they have to be, the bound alone decides.
A program may use at most 64 MiB of HBM per device.

v0:
```python
import functools
import math

import jax
import jax.numpy as jnp
from jax import lax
from jax.experimental import pallas as pl
from jax.experimental.pallas import tpu as pltpu
from jax.sharding import PartitionSpec as P

MESH = pl.DeviceIdType.MESH
VMEM = pltpu.VMEM
CHUNKS = 3
PAIR = 2
ROWS = 12
ANGLES = 96
f32, bf16 = jnp.float32, jnp.bfloat16


def split(x):
    high = x.astype(bf16)
    return high, (x - high.astype(f32)).astype(bf16)


def dot3(a, b, dims):
    def one(u, v):
        return lax.dot_general(u, v, (dims, ((), ())), preferred_element_type=f32)

    return one(a[0], b[0]) + (one(a[0], b[1]) + one(a[1], b[0]))


NN = ((1,), (0,))
NT = ((1,), (1,))


def lane(shape):
    return lax.broadcasted_iota(jnp.int32, shape, len(shape) - 1)


def sub(shape):
    return lax.broadcasted_iota(jnp.int32, shape, 0)


def lroll(x, n):
    return pltpu.roll(x, n, 1)


def sroll(x):
    return pltpu.roll(x, 4, 0)


def phase(half):
    s = half * half
    c = 1.0 / 479001600.0
    for k in (-1.0 / 3628800.0, 1.0 / 40320.0, -1.0 / 720.0, 1.0 / 24.0, -0.5, 1.0):
        c = c * s + k
    v = -1.0 / 39916800.0
    for k in (1.0 / 362880.0, -1.0 / 5040.0, 1.0 / 120.0, -1.0 / 6.0, 1.0):
        v = v * s + k
    return c, v * half


def spread(v0, v1, v2):
    n = lane(v0.shape)
    return (
        v0,
        lroll(jnp.where(n >= 96, v0, v1), 32),
        lroll(jnp.where(n >= 64, v1, v2), 64),
        lroll(v2, 96),
    )


def dense(b0, b1, b2, b3):
    n = lane(b0.shape)
    r1, r2, r3 = lroll(b1, 96), lroll(b2, 64), lroll(b3, 32)
    return jnp.where(n < 96, b0, r1), jnp.where(n < 64, r1, r2), jnp.where(n < 32, r2, r3)


def dense_half(u0, u1):
    n = lane(u0.shape)
    r = lroll(u1, 96)
    tail = jnp.where(n < 64, r, sroll(lroll(r, 64)))
    return jnp.where(n < 96, u0, r), tail[0:4]


def tail_rows(tail):
    both = jnp.concatenate([tail, tail], axis=0)
    return jnp.where(sub(both.shape) < 4, both, lroll(both, 64))


def spread_half(tile, tail):
    n = lane(tile.shape)
    return tile, lroll(jnp.where(n >= 96, tile, tail_rows(tail)), 32)


def angle_lanes(values):
    n = lane(values[0].shape[:-1] + (128,))
    a, b, c, d = values
    return jnp.where(n < 96, a, b), jnp.where(n < 64, b, c), jnp.where(n < 32, c, d)


def before_kernel(groups, wave, pot, ar, ab, bond, main, tail, pots, bigw, mat_hi, mat_lo):
    bonds = 4 * groups
    blocks = 3 * groups

    def turn(k, _):
        at = pl.ds(pl.multiple_of(k * 128, 128), 128)
        pots[pl.ds(k, 8, stride=blocks), :] = pot[0:8, at]
        pots[pl.ds(8 * blocks + k, 4, stride=blocks), :] = pot[8:12, at]
        return 0

    lax.fori_loop(0, blocks, turn, 0, unroll=4)

    place = lax.broadcasted_iota(jnp.int32, (bonds, bonds), 1)
    point = lax.broadcasted_iota(jnp.int32, (bonds, bonds), 0)
    perm = jnp.where(point == 4 * (place % groups) + place // groups, 1.0, 0.0).astype(bf16)
    for c in range(2):
        for part, mat in zip(split(bond[c]), (mat_hi, mat_lo)):
            cols = jnp.dot(part, perm, preferred_element_type=f32).astype(bf16)
            rows = lax.dot_general(perm, cols, (((0,), (0,)), ((), ())), preferred_element_type=f32)
            rows = rows.astype(bf16)
            if c == 0:
                mat[0:bonds, 0:bonds] = rows
                mat[bonds:, bonds:] = rows
            else:
                mat[0:bonds, bonds:] = -rows
                mat[bonds:, 0:bonds] = rows

    grid = (groups, bonds)
    cols = []
    for i in range(4):
        mine = jnp.where(lane(grid) == 4 * sub(grid) + i, jnp.broadcast_to(ab[...], grid), 0.0)
        cols.append(jnp.exp(-0.5 * jnp.sum(mine, axis=1, keepdims=True)))
    damp = angle_lanes([jnp.broadcast_to(c, (groups, 128)) for c in cols])
    decay = jnp.exp(-0.5 * ar[...])

    def two_rows(h, _):
        sides = []
        for k in range(2):
            r = 2 * h + k
            own = jnp.sum(jnp.where(lane((1, 128)) == r, decay, 0.0), axis=1, keepdims=True)
            re, im = [], []
            for i in range(3):
                x = wave[pl.ds(r * 2 * blocks + 2 * i, groups, stride=6), :]
                y = wave[pl.ds(r * 2 * blocks + 2 * i + 1, groups, stride=6), :]
                co, si = phase(0.5 * pots[pl.ds(r * blocks + i, groups, stride=3), :])
                d = damp[i] * own
                co, si = d * co, d * si
                re.append(co * x + si * y)
                im.append(co * y - si * x)
            sides.append(jnp.concatenate(spread(*re) + spread(*im), axis=0))
        x = jnp.concatenate(sides, axis=1)
        x = x + dot3((mat_hi[...], mat_lo[...]), split(x), NN)
        for k in range(2):
            r = 2 * h + k
            for c in range(2):
                row = jnp.where(r < 8, r + 8 * c, r + 8 + 4 * c)
                for i in range(4):
                    at = (4 * c + i) * groups
                    bigw[pl.ds(24 * i + row, groups, stride=96), :] = x[at : at + groups, 128 * k : 128 * k + 128]
        return 0

    lax.fori_loop(0, ROWS // 2, two_rows, 0)

    def pack(p, _):
        w = [[bigw[pl.ds(pl.multiple_of((2 * p + b) * 24, 8) + 8 * k, 8), :] for k in range(3)] for b in range(2)]
        t = dense(w[0][0], w[1][0], w[0][1], w[1][1])
        last, rest = dense_half(w[0][2], w[1][2])
        for k in range(3):
            main[p, 8 * k : 8 * k + 8, :] = t[k]
        main[p, 24:32, :] = last
        tail[p] = rest
        return 0

    lax.fori_loop(0, bonds // 2, pack, 0, unroll=2)


def turn_kernel(
    nz, top, sent_m, sent_t, weight, angle, ladder, radial, back_m, back_t,
    got_m, got_t, got_w, own_w, wide, work, from_up, from_down, reply_m, reply_t,
    a_hi, a_lo, u_hi, u_lo, d_hi, d_lo, r_hi, r_lo, scratch,
    angles, sa_sem, ra_sem, s1m, s1t, s1w, r1m, r1t, r1w, su, sd, ru, rd, s2m, s2t, r2m, r2t,
):
    owners = 4 * nz
    ka, sa = lax.axis_index("ka"), lax.axis_index("sa")
    x, yh = ka // 2, ka % 2
    yl, z, core = sa // (2 * nz), (sa // 2) % nz, sa % 2
    y = 2 * yh + yl
    helicity = 2 * x + core
    me_owner = y * nz + z
    at_home = core == yh

    def owner_of(q, c):
        oy, oz = q // nz, q % nz
        return (2 * x + oy // 2, (oy % 2) * (2 * nz) + oz * 2 + c)

    def home_of(s):
        return (2 * x + core, s)

    def turned(i):
        return ((y + i % 4) % 4) * nz + (z + nz // 2 + i // 4) % nz

    def turned_home(i):
        c, iy, iz = i % 2, (i // 2) % 2, i // 4
        return ((yl + iy) % 2) * (2 * nz) + ((z + nz // 2 + iz) % nz) * 2 + c

    has_up, has_down = helicity < top, helicity > 0
    kx_up = jnp.where(core == 0, x, x + 1)
    kx_down = jnp.where(core == 1, x, x - 1)
    up_dev = (2 * kx_up + yh, yl * (2 * nz) + z * 2 + 1 - core)
    down_dev = (2 * kx_down + yh, yl * (2 * nz) + z * 2 + 1 - core)

    barrier = pltpu.get_barrier_semaphore()

    def greet(i, _):
        q, s = turned(i), turned_home(i)

        @pl.when(jnp.logical_not(at_home & (q == me_owner)))
        def _():
            pl.semaphore_signal(barrier, inc=1, device_id=owner_of(q, yh), device_id_type=MESH)

        @pl.when(jnp.logical_not(at_home & (s == sa)))
        def _():
            pl.semaphore_signal(barrier, inc=1, device_id=home_of(s), device_id_type=MESH)

        return 0

    lax.fori_loop(0, owners, greet, 0)

    @pl.when(has_up)
    def _():
        pl.semaphore_signal(barrier, inc=1, device_id=up_dev, device_id_type=MESH)

    @pl.when(has_down)
    def _():
        pl.semaphore_signal(barrier, inc=1, device_id=down_dev, device_id_type=MESH)

    own_w[...] = weight[...]

    expected = 2 * owners - 2 * at_home.astype(jnp.int32)
    expected = expected + has_up.astype(jnp.int32) + has_down.astype(jnp.int32)
    pl.semaphore_wait(barrier, expected)

    def send_chunk(j, src_m, src_t, dst_m, dst_t, pick, device, slot, ssm, sst, rsm, rst, self_slot):
        def one(i, _):
            q = pick(i)
            mine = at_home & (q == self_slot)
            here = [
                (src_m.at[j * owners + q], dst_m.at[j * owners + slot], ssm.at[j], rsm.at[j]),
                (src_t.at[j * owners + q], dst_t.at[j * owners + slot], sst.at[j], rst.at[j]),
            ]

            @pl.when(mine)
            def _():
                for a, b, _, r in here:
                    pltpu.make_async_copy(a, b, r).start()

            @pl.when(jnp.logical_not(mine))
            def _():
                for a, b, s, r in here:
                    pltpu.make_async_remote_copy(
                        src_ref=a, dst_ref=b, send_sem=s, recv_sem=r, device_id=device(q), device_id_type=MESH
                    ).start()

            return 0

        lax.fori_loop(0, owners, one, 0)

    def send_weight(i, _):
        q = turned(i)
        mine = at_home & (q == me_owner)

        @pl.when(mine)
        def _():
            pltpu.make_async_copy(own_w, got_w.at[sa], r1w).start()

        @pl.when(jnp.logical_not(mine))
        def _():
            pltpu.make_async_remote_copy(
                src_ref=own_w, dst_ref=got_w.at[sa], send_sem=s1w, recv_sem=r1w,
                device_id=owner_of(q, yh), device_id_type=MESH,
            ).start()

        return 0

    def wait_bytes(ref, count, start, sem):
        view = ref.at[pl.ds(start, count)]
        pltpu.make_async_copy(view, view, sem).wait()

    def wait_sent(ref, start, sem):
        @pl.when(at_home)
        def _():
            wait_bytes(ref, owners - 1, start, sem)

        @pl.when(jnp.logical_not(at_home))
        def _():
            wait_bytes(ref, owners, start, sem)

    to_other = pltpu.make_async_remote_copy(
        src_ref=angle, dst_ref=angles, send_sem=sa_sem, recv_sem=ra_sem,
        device_id=(2 * x + 1 - yh, sa), device_id_type=MESH,
    )

    @pl.when(at_home)
    def _():
        to_other.start()
        angles[...] = angle[...]

    lax.fori_loop(0, owners, send_weight, 0)
    for j in range(CHUNKS):
        send_chunk(
            j, sent_m, sent_t, got_m, got_t, turned, lambda q: owner_of(q, yh), sa, s1m, s1t, r1m, r1t, me_owner
        )

    def fill(parts, hi, lo, shape):
        scratch[0 : shape[0], 0 : shape[1]] = jnp.zeros(shape, f32)
        for row, col, value in parts:
            scratch[row : row + ANGLES, col : col + ANGLES] = value
        high, low = split(scratch[0 : shape[0], 0 : shape[1]])
        hi[...] = high
        lo[...] = low

    coef_up, coef_down = 0.0, 0.0
    for k in range(top + 1):
        coef_up = jnp.where(helicity == k, math.sqrt(top * (top + 1) - k * (k + 1)), coef_up)
        coef_down = jnp.where(helicity == k, math.sqrt(top * (top + 1) - (k - 1) * k), coef_down)
    up = coef_up * ladder[...]
    down = coef_down * ladder[...]
    fill([(0, 128, up), (128, 0, -up)], u_hi, u_lo, (256, 256))
    fill([(128, 0, down), (0, 128, -down)], d_hi, d_lo, (256, 256))
    count = radial.shape[1]
    for c in range(2):
        high, low = split(radial[c])
        for part, mat in ((high, r_hi), (low, r_lo)):
            if c == 0:
                mat[0:count, 0:count] = part
                mat[count:, count:] = part
            else:
                mat[0:count, count:] = -part
                mat[count:, 0:count] = part

    for buf, has in ((from_up, has_up), (from_down, has_down)):

        @pl.when(jnp.logical_not(has))
        def _(buf=buf):
            buf[...] = jnp.zeros(buf.shape, f32)

    @pl.when(jnp.logical_not(at_home))
    def _():
        to_other.wait_recv()

    fill(
        [(0, 0, angles[0, 0]), (128, 128, angles[0, 0]), (0, 128, -angles[0, 1]), (128, 0, angles[0, 1])],
        a_hi, a_lo, (256, 256),
    )
    wait_bytes(got_w, owners, 0, r1w)

    def weights(sp, _):
        shape = (2 * ROWS, 128)
        row = sub(shape)
        a = jnp.where(row < ROWS, got_w[2 * sp], got_w[2 * sp + 1])
        a = jnp.where(lane(shape) == jnp.where(row < ROWS, row, row - ROWS), a, 0.0)
        at = pl.ds(pl.multiple_of(sp * 2 * ROWS, 8), 2 * ROWS)
        wide[at, :] = jnp.broadcast_to(jnp.sum(a, axis=1, keepdims=True), shape)
        return 0

    lax.fori_loop(0, owners // 2, weights, 0)

    for j in range(CHUNKS):
        wait_bytes(got_m, owners, j * owners, r1m.at[j])
        wait_bytes(got_t, owners, j * owners, r1t.at[j])

        def unpack(sp, _, j=j):
            top8 = sub((8, 128)) < 4
            got = []
            for k in range(2):
                s = j * owners + 2 * sp + k
                t = [got_m[s, 8 * i : 8 * i + 8, :] for i in range(4)]
                re0, re1, im0, im1 = spread(t[0], t[1], t[2])
                u0, u1 = spread_half(t[3], got_t[s])
                got.append(((re0, im0, u0), (re1, im1, u1)))
            base = pl.multiple_of(sp * 24, 8)
            for b in range(2):
                (re_a, im_a, u_a), (re_b, im_b, u_b) = got[0][b], got[1][b]
                re_b, im_b = sroll(re_b), sroll(im_b)
                tiles = (
                    (re_a, jnp.where(top8, u_a, re_b), jnp.where(top8, re_b, sroll(u_b))),
                    (im_a, jnp.where(top8, sroll(u_a), im_b), jnp.where(top8, im_b, u_b)),
                )
                for c in range(2):
                    for i in range(3):
                        work[j, b, pl.ds(base + 8 * i, 8), 128 * c : 128 * c + 128] = tiles[c][i]
            return 0

        lax.fori_loop(0, owners // 2, unpack, 0)
        for b in range(2):
            v = work[j, b]
            work[j, b] = v + dot3(split(v), (a_hi[...], a_lo[...]), NT)

        @pl.when(has_up)
        def _(j=j):
            pltpu.make_async_remote_copy(
                src_ref=work.at[j], dst_ref=from_down.at[j], send_sem=su.at[j], recv_sem=rd.at[j],
                device_id=up_dev, device_id_type=MESH,
            ).start()

        @pl.when(has_down)
        def _(j=j):
            pltpu.make_async_remote_copy(
                src_ref=work.at[j], dst_ref=from_up.at[j], send_sem=sd.at[j], recv_sem=ru.at[j],
                device_id=down_dev, device_id_type=MESH,
            ).start()

        @pl.when(has_up)
        def _(j=j):
            pltpu.make_async_copy(from_up.at[j], from_up.at[j], ru.at[j]).wait()

        @pl.when(has_down)
        def _(j=j):
            pltpu.make_async_copy(from_down.at[j], from_down.at[j], rd.at[j]).wait()

        third = []
        for b in range(2):
            c = dot3(split(from_up[j, b]), (u_hi[...], u_lo[...]), NT)
            c = c + dot3(split(from_down[j, b]), (d_hi[...], d_lo[...]), NN)
            w = wide[...]
            third.append(work[j, b] + jnp.concatenate([w, w], axis=1) * c)
        v = jnp.concatenate(
            [
                jnp.concatenate([third[0][:, 0:128], third[1][:, 0:128]], axis=1),
                jnp.concatenate([third[0][:, 128:256], third[1][:, 128:256]], axis=1),
            ],
            axis=0,
        )
        scratch[...] = v + dot3((r_hi[...], r_lo[...]), split(v), NN)

        def repack(sp, _, j=j):
            top8 = sub((8, 128)) < 4
            base = pl.multiple_of(sp * 24, 8)
            out = [[], []]
            for b in range(2):
                (a0, a1, a2), (i0, i1, i2) = [
                    [scratch[pl.ds(base + c * count + 8 * i, 8), 128 * b : 128 * b + 128] for i in range(3)]
                    for c in range(2)
                ]
                r1, r2, q1, q2 = sroll(a1), sroll(a2), sroll(i1), sroll(i2)
                out[0].append((a0, i0, jnp.where(top8, a1, q1)))
                out[1].append((jnp.where(top8, r1, r2), jnp.where(top8, q1, q2), jnp.where(top8, r2, i2)))
            for k in range(2):
                s = j * owners + 2 * sp + k
                (re0, im0, u0), (re1, im1, u1) = out[k]
                t = dense(re0, re1, im0, im1)
                last, rest = dense_half(u0, u1)
                for i in range(3):
                    reply_m[s, 8 * i : 8 * i + 8, :] = t[i]
                reply_m[s, 24:32, :] = last
                reply_t[s] = rest
            return 0

        lax.fori_loop(0, owners // 2, repack, 0)
        send_chunk(
            j, reply_m, reply_t, back_m, back_t, turned_home, home_of, me_owner, s2m, s2t, r2m, r2t, sa
        )

    @pl.when(at_home)
    def _():
        to_other.wait_send()

    wait_sent(got_w, 0, s1w)
    for j in range(CHUNKS):
        wait_sent(sent_m, j * owners, s1m.at[j])
        wait_sent(sent_t, j * owners, s1t.at[j])

        @pl.when(has_up)
        def _(j=j):
            pltpu.make_async_copy(work.at[j], work.at[j], su.at[j]).wait()

        @pl.when(has_down)
        def _(j=j):
            pltpu.make_async_copy(work.at[j], work.at[j], sd.at[j]).wait()

    for j in range(CHUNKS):
        wait_bytes(back_m, owners, j * owners, r2m.at[j])
        wait_bytes(back_t, owners, j * owners, r2t.at[j])
        wait_sent(reply_m, j * owners, s2m.at[j])
        wait_sent(reply_t, j * owners, s2t.at[j])


def after_kernel(groups, main, tail, pot, ar, ab, out):
    blocks = 3 * groups
    row8 = sub((8, 1))
    decay8, decay4 = jnp.zeros((8, 1), f32), jnp.zeros((8, 1), f32)
    for k in range(8):
        decay8 = jnp.where(row8 == k, ar[k], decay8)
        decay4 = jnp.where(row8 % 4 == k % 4, ar[8 + k % 4], decay4)

    def group(g, _):
        points = [jnp.full((8, 128), ab[4 * g + i], f32) for i in range(4)]
        flat = angle_lanes(points)
        a, b = 2 * g, 2 * g + 1
        ta = [main[a, 8 * i : 8 * i + 8, :] for i in range(4)]
        tb = [main[b, 8 * i : 8 * i + 8, :] for i in range(4)]
        low = lane((8, 128)) < 64
        b0, b1, b3 = lroll(tb[0], 64), lroll(tb[1], 64), lroll(tb[3], 64)
        a1, a2 = lroll(ta[1], 64), lroll(ta[2], 64)
        re = (ta[0], jnp.where(low, ta[1], b0), jnp.where(low, b0, b1))
        im = (jnp.where(low, a1, a2), jnp.where(low, a2, tb[1]), tb[2])
        ra, rb = tail_rows(tail[a]), tail_rows(tail[b])
        u = (ta[3], jnp.where(low, ra, b3), jnp.where(low, b3, lroll(rb, 64)))
        top = sub((8, 128)) < 4
        for i in range(3):
            k = 3 * g + i
            at = pl.ds(pl.multiple_of(k * 128, 128), 128)
            co, si = phase(0.5 * pot[0:8, at])
            d = jnp.exp(-0.5 * (decay8 + flat[i]))
            co, si = d * co, d * si
            out[pl.ds(2 * k, 8, stride=2 * blocks), :] = co * re[i] + si * im[i]
            out[pl.ds(2 * k + 1, 8, stride=2 * blocks), :] = co * im[i] - si * re[i]
            p4 = pot[8:12, at]
            co, si = phase(0.5 * jnp.concatenate([p4, p4], axis=0))
            d = jnp.exp(-0.5 * (decay4 + flat[i]))
            co, si = d * co, d * si
            v = co * u[i] + jnp.where(top, si, -si) * sroll(u[i])
            out[pl.ds(16 * blocks + 2 * k, 4, stride=2 * blocks), :] = v[0:4]
            out[pl.ds(16 * blocks + 2 * k + 1, 4, stride=2 * blocks), :] = v[4:8]
        return 0

    lax.fori_loop(0, groups, group, 0)


def body(wave_in, potential, absorb_radial, absorb_bond, coriolis_weight, ladder, angle_step, bond_step, radial_step):
    rows, columns = wave_in.shape[2:]
    blocks = columns // 128
    groups = blocks // 3
    nz = lax.axis_size("sa") // 4
    owners = 4 * nz
    top = lax.axis_size("ka") - 1
    count = radial_step.shape[1]
    full = pl.BlockSpec(memory_space=VMEM)
    smem = pl.BlockSpec(memory_space=pltpu.SMEM)
    hbm = pl.BlockSpec(memory_space=pl.ANY)
    shape = jax.ShapeDtypeStruct
    wave = wave_in.reshape(2, rows, blocks, 128).transpose(1, 2, 0, 3).reshape(rows * blocks * 2, 128)
    pad = jnp.pad(absorb_radial, (0, 128 - rows)).reshape(1, 128)
    weight = jnp.pad(coriolis_weight, (0, 128 - rows)).reshape(1, 128)
    messages = CHUNKS * owners
    main, tail = pl.pallas_call(
        functools.partial(before_kernel, groups),
        out_shape=(shape((messages, 32, 128), f32), shape((messages, 4, 128), f32)),
        in_specs=[full] * 5,
        out_specs=(full, full),
        scratch_shapes=[
            VMEM((rows * blocks, 128), f32),
            VMEM((96 * groups, 128), f32),
            VMEM((8 * groups, 8 * groups), bf16),
            VMEM((8 * groups, 8 * groups), bf16),
        ],
        compiler_params=pltpu.CompilerParams(vmem_limit_bytes=50 << 20),
        name="before",
    )(wave, potential, pad, absorb_bond.reshape(1, -1), bond_step)
    dma, many = pltpu.SemaphoreType.DMA, pltpu.SemaphoreType.DMA((CHUNKS,))
    back_m, back_t = pl.pallas_call(
        functools.partial(turn_kernel, nz, top),
        out_shape=(shape((messages, 32, 128), f32), shape((messages, 4, 128), f32)),
        in_specs=[hbm, hbm, full, full, full, full],
        out_specs=(hbm, hbm),
        scratch_shapes=[
            VMEM((messages, 32, 128), f32),
            VMEM((messages, 4, 128), f32),
            VMEM((owners, 1, 128), f32),
            VMEM((1, 128), f32),
            VMEM((count, 128), f32),
            VMEM((CHUNKS, 2, count, 256), f32),
            VMEM((CHUNKS, 2, count, 256), f32),
            VMEM((CHUNKS, 2, count, 256), f32),
            VMEM((messages, 32, 128), f32),
            VMEM((messages, 4, 128), f32),
            VMEM((256, 256), bf16),
            VMEM((256, 256), bf16),
            VMEM((256, 256), bf16),
            VMEM((256, 256), bf16),
            VMEM((256, 256), bf16),
            VMEM((256, 256), bf16),
            VMEM((2 * count, 2 * count), bf16),
            VMEM((2 * count, 2 * count), bf16),
            VMEM((2 * count, 256), f32),
            VMEM((1, 2, ANGLES, ANGLES), f32), dma, dma,
            many, many, dma, many, many, dma,
            many, many, many, many,
            many, many, many, many,
        ],
        compiler_params=pltpu.CompilerParams(collective_id=0, has_side_effects=True, vmem_limit_bytes=50 << 20),
        name="turn",
    )(main, tail, weight, angle_step, ladder, radial_step)
    out = pl.pallas_call(
        functools.partial(after_kernel, groups),
        out_shape=shape((rows * blocks * 2, 128), f32),
        in_specs=[full, full, full, smem, smem],
        out_specs=full,
        compiler_params=pltpu.CompilerParams(vmem_limit_bytes=50 << 20),
        name="after",
    )(back_m, back_t, potential, absorb_radial, absorb_bond)
    return out.reshape(rows, blocks, 2, 128).transpose(2, 0, 1, 3).reshape(1, 2, rows, columns)


def solution(mesh):
    return jax.shard_map(
        body,
        mesh=mesh,
        in_specs=(
            P("ka", None, "sa", None),
            P("sa", None),
            P("sa"),
            P(),
            P("sa"),
            P(),
            P("ka", None, None, None),
            P(),
            P(),
        ),
        out_specs=P("ka", None, "sa", None),
        check_vma=False,
    )
```

profile of v0, /device:TPU:69, one launch (start us, length us, event | category | flops | bytes accessed | tf_op | source)
XLA Modules:
  0.0 132.6 jit_solution(11198897478025676174)
XLA Ops:
  0.0 0.7 pad_bitcast_fusion.weight
  0.7 0.7 pad_bitcast_fusion.1.ar
  1.3 0.0 copy-start
  1.3 1.3 copy-done
  2.6 0.0 copy-start.4
  2.6 1.0 copy-done.4
  3.6 0.0 copy-start.7
  3.6 0.7 copy-done.7
  4.3 0.0 copy-start.3
  4.3 0.0 copy-start.5
  4.3 0.0 copy-start.6
  4.3 15.6 %before.1 = (f32[96,32,128]{2,1,0:T(8,128)S(1)}, f32[96,4,128]{2,1,0:T(4,128)S(1)}) custom-call(f32[3456,128]{1,0:T(8,128)} %bitcast.16, f32[12,18432]{1,0:T(8,128)S(1)} %copy-done, f32[1,128]{1,0:T(1,128)S(1)} %pad_bitcast_fusion.1.ar, f32[1,192]{1,0:T(1,128)S(1)} %bitcast.15, f32[2,192,192]{2,1,0:T(8,128)S(1)} %copy-done.4), custom_call_target="tpu_custom_call" | custom-call | tf_op jit(solution)/shard_map/before/pallas_call | solution.py:547
  19.9 0.0 copy-start.2
  19.9 1.1 copy-done.2
  21.0 0.0 copy-start.1
  21.0 0.0 copy-start.8
  21.0 0.0 copy-done.3
  21.0 0.0 copy-done.5
  21.0 0.0 copy-done.6
  21.0 102.5 %turn.1 = (f32[96,32,128]{2,1,0:T(8,128)S(1)}, f32[96,4,128]{2,1,0:T(4,128)S(1)}) custom-call(f32[96,32,128]{2,1,0:T(8,128)} %copy-done.2, f32[96,4,128]{2,1,0:T(4,128)S(1)} %get-tuple-element.10.sent_t, f32[1,128]{1,0:T(1,128)S(1)} %pad_bitcast_fusion.weight, f32[1,2,96,96]{3,2,1,0:T(8,128)S(1)} %copy-done.5, f32[96,96]{1,0:T(8,128)S(1)} %copy-done.6, ...), custom_call_target="tpu_custom_call" | custom-call | tf_op jit(solution)/shard_map/turn/pallas_call | solution.py:562
  123.5 0.0 copy-done.1
  123.5 0.0 copy-done.8
  123.5 9.1 %after.1 = f32[3456,128]{1,0:T(8,128)} custom-call(f32[96,32,128]{2,1,0:T(8,128)S(1)} %get-tuple-element.11.main, f32[96,4,128]{2,1,0:T(4,128)S(1)} %get-tuple-element.12.tail, f32[12,18432]{1,0:T(8,128)S(1)} %copy-done.1, f32[12]{0:T(128)S(1)} %copy-done.8, f32[192]{0:T(256)S(1)} %copy-done.7), custom_call_target="tpu_custom_call" | custom-call | tf_op jit(solution)/shard_map/after/pallas_call | solution.py:595
Async XLA Ops:
  1.3 1.3 copy-start
  2.6 1.0 copy-start.4
  3.6 0.7 copy-start.7
  4.3 16.7 %copy-start.3 = (f32[2,384,384]{2,1,0:T(8,128)S(1)}, f32[2,384,384]{2,1,0:T(8,128)}, u32[]{:S(2)}) copy-start(f32[2,384,384]{2,1,0:T(8,128)} %radial.1) | copy-start | bytes 3538948
  4.3 16.7 %copy-start.5 = (f32[1,2,96,96]{3,2,1,0:T(8,128)S(1)}, f32[1,2,96,96]{3,2,1,0:T(8,128)}, u32[]{:S(2)}) copy-start(f32[1,2,96,96]{3,2,1,0:T(8,128)} %angle.1) | copy-start | bytes 221188
  4.3 16.8 %copy-start.6 = (f32[96,96]{1,0:T(8,128)S(1)}, f32[96,96]{1,0:T(8,128)}, u32[]{:S(2)}) copy-start(f32[96,96]{1,0:T(8,128)} %ladder.1) | copy-start | bytes 110596
  19.9 1.2 copy-start.2
  21.0 102.5 %copy-start.1 = (f32[12,18432]{1,0:T(8,128)S(1)}, f32[12,18432]{1,0:T(8,128)}, u32[]{:S(2)}) copy-start(f32[12,18432]{1,0:T(8,128)} %pot.3) | copy-start | bytes 2654212
  21.0 102.5 %copy-start.8 = (f32[12]{0:T(128)S(1)}, f32[12]{0:T(128)}, u32[]{:S(2)}) copy-start(f32[12]{0:T(128)} %ar.1) | copy-start | bytes 148
where the time goes:
time: 133 us
  Pallas kernels  127 us (95%)
  local copies, waits for them, and re-layouts  5.43 us (4%)
    pallas_call x1, Pallas kernels, body(): pl.pallas_call(functools.partial(turn_kernel, nz, top), out_shape=(shape(...  102 us
    pallas_call x1, Pallas kernels, body(): pl.pallas_call(functools.partial(before_kernel, groups), out_shape=(shape...  15.6 us
    pallas_call x1, Pallas kernels, body(): pl.pallas_call(functools.partial(after_kernel, groups), out_shape=shape((...  9.12 us
    unnamed x18, local copies, waits for them, and re-layouts  4.11 us

commit v1 on v0

--- a/solution.py
+++ b/solution.py
@@ -14,6 +14,8 @@
 PAIR = 2
 ROWS = 12
 ANGLES = 96
+PACK = 4
+GATES = 4
 f32, bf16 = jnp.float32, jnp.bfloat16
 
 
@@ -102,11 +104,12 @@
 def before_kernel(groups, wave, pot, ar, ab, bond, main, tail, pots, bigw, mat_hi, mat_lo):
     bonds = 4 * groups
     blocks = 3 * groups
+    pitch = blocks + 1
 
     def turn(k, _):
         at = pl.ds(pl.multiple_of(k * 128, 128), 128)
-        pots[pl.ds(k, 8, stride=blocks), :] = pot[0:8, at]
-        pots[pl.ds(8 * blocks + k, 4, stride=blocks), :] = pot[8:12, at]
+        pots[pl.ds(k, 8, stride=pitch), :] = pot[0:8, at]
+        pots[pl.ds(8 * pitch + k, 4, stride=pitch), :] = pot[8:12, at]
         return 0
 
     lax.fori_loop(0, blocks, turn, 0, unroll=4)
@@ -143,7 +146,7 @@
             for i in range(3):
                 x = wave[pl.ds(r * 2 * blocks + 2 * i, groups, stride=6), :]
                 y = wave[pl.ds(r * 2 * blocks + 2 * i + 1, groups, stride=6), :]
-                co, si = phase(0.5 * pots[pl.ds(r * blocks + i, groups, stride=3), :])
+                co, si = phase(0.5 * pots[pl.ds(r * pitch + i, groups, stride=3), :])
                 d = damp[i] * own
                 co, si = d * co, d * si
                 re.append(co * x + si * y)
@@ -157,22 +160,27 @@
                 row = jnp.where(r < 8, r + 8 * c, r + 8 + 4 * c)
                 for i in range(4):
                     at = (4 * c + i) * groups
-                    bigw[pl.ds(24 * i + row, groups, stride=96), :] = x[at : at + groups, 128 * k : 128 * k + 128]
+                    bigw[pl.ds(i + 5 * row, groups, stride=121), :] = x[at : at + groups, 128 * k : 128 * k + 128]
         return 0
 
-    lax.fori_loop(0, ROWS // 2, two_rows, 0)
-
-    def pack(p, _):
-        w = [[bigw[pl.ds(pl.multiple_of((2 * p + b) * 24, 8) + 8 * k, 8), :] for k in range(3)] for b in range(2)]
-        t = dense(w[0][0], w[1][0], w[0][1], w[1][1])
-        last, rest = dense_half(w[0][2], w[1][2])
-        for k in range(3):
-            main[p, 8 * k : 8 * k + 8, :] = t[k]
-        main[p, 24:32, :] = last
-        tail[p] = rest
+    lax.fori_loop(0, ROWS // 2, two_rows, 0, unroll=True)
+
+    def pack(h, _):
+        pairs = [PACK * h + k for k in range(PACK)]
+        loaded = [
+            [bigw[pl.ds(121 * (p // 2) + 2 * (p % 2) + b + 40 * k, 8, stride=5), :] for b in range(2) for k in range(3)]
+            for p in pairs
+        ]
+        made = [
+            (*dense(w[0], w[3], w[1], w[4]), *dense_half(w[2], w[5])) for w in loaded
+        ]
+        for p, t in zip(pairs, made):
+            for k in range(4):
+                main[p, 8 * k : 8 * k + 8, :] = t[k]
+            tail[p] = t[4]
         return 0
 
-    lax.fori_loop(0, bonds // 2, pack, 0, unroll=2)
+    lax.fori_loop(0, bonds // 2 // PACK, pack, 0, unroll=2)
 
 
 def turn_kernel(
@@ -241,12 +249,12 @@
     expected = expected + has_up.astype(jnp.int32) + has_down.astype(jnp.int32)
     pl.semaphore_wait(barrier, expected)
 
-    def send_chunk(j, src_m, src_t, dst_m, dst_t, pick, device, slot, ssm, sst, rsm, rst, self_slot):
+    def send_chunk(j, part, src_m, src_t, dst_m, dst_t, pick, device, slot, ssm, sst, rsm, rst, self_slot):
         def one(i, _):
             q = pick(i)
             mine = at_home & (q == self_slot)
             here = [
-                (src_m.at[j * owners + q], dst_m.at[j * owners + slot], ssm.at[j], rsm.at[j]),
+                (src_m.at[j * owners + q], dst_m.at[j * owners + slot], ssm, rsm.at[j]),
                 (src_t.at[j * owners + q], dst_t.at[j * owners + slot], sst.at[j], rst.at[j]),
             ]
 
@@ -264,7 +272,7 @@
 
             return 0
 
-        lax.fori_loop(0, owners, one, 0)
+        lax.fori_loop(*part, one, 0)
 
     def send_weight(i, _):
         q = turned(i)
@@ -307,10 +315,37 @@
         angles[...] = angle[...]
 
     lax.fori_loop(0, owners, send_weight, 0)
-    for j in range(CHUNKS):
+    size = owners // GATES
+    mine_at = (nz // 2) * 4 // size
+
+    def first_send(j, k):
         send_chunk(
-            j, sent_m, sent_t, got_m, got_t, turned, lambda q: owner_of(q, yh), sa, s1m, s1t, r1m, r1t, me_owner
+            j, (k * size, k * size + size), sent_m, sent_t, got_m, got_t, turned, lambda q: owner_of(q, yh), sa,
+            s1m.at[j, k], s1t, r1m, r1t, me_owner,
         )
+
+    def gate(j, k):
+        if k != mine_at:
+            wait_bytes(sent_m, size, 0, s1m.at[j, k])
+        else:
+
+            @pl.when(at_home)
+            def _():
+                wait_bytes(sent_m, size - 1, 0, s1m.at[j, k])
+
+            @pl.when(jnp.logical_not(at_home))
+            def _():
+                wait_bytes(sent_m, size, 0, s1m.at[j, k])
+
+    def advance(j, parts):
+        for k in parts:
+            if j < CHUNKS:
+                gate(j, k)
+            if j + 1 < CHUNKS:
+                first_send(j + 1, k)
+
+    for k in range(GATES):
+        first_send(0, k)
 
     def fill(parts, hi, lo, shape):
         scratch[0 : shape[0], 0 : shape[1]] = jnp.zeros(shape, f32)
@@ -366,57 +401,63 @@
 
     lax.fori_loop(0, owners // 2, weights, 0)
 
-    for j in range(CHUNKS):
+    def receive(j):
         wait_bytes(got_m, owners, j * owners, r1m.at[j])
         wait_bytes(got_t, owners, j * owners, r1t.at[j])
 
-        def unpack(sp, _, j=j):
+        def unpack(h, _):
             top8 = sub((8, 128)) < 4
+            loaded = [
+                [got_m[j * owners + 4 * h + k, 8 * i : 8 * i + 8, :] for i in range(4)] + [got_t[j * owners + 4 * h + k]]
+                for k in range(4)
+            ]
             got = []
-            for k in range(2):
-                s = j * owners + 2 * sp + k
-                t = [got_m[s, 8 * i : 8 * i + 8, :] for i in range(4)]
+            for t in loaded:
                 re0, re1, im0, im1 = spread(t[0], t[1], t[2])
-                u0, u1 = spread_half(t[3], got_t[s])
+                u0, u1 = spread_half(t[3], t[4])
                 got.append(((re0, im0, u0), (re1, im1, u1)))
-            base = pl.multiple_of(sp * 24, 8)
-            for b in range(2):
-                (re_a, im_a, u_a), (re_b, im_b, u_b) = got[0][b], got[1][b]
-                re_b, im_b = sroll(re_b), sroll(im_b)
-                tiles = (
-                    (re_a, jnp.where(top8, u_a, re_b), jnp.where(top8, re_b, sroll(u_b))),
-                    (im_a, jnp.where(top8, sroll(u_a), im_b), jnp.where(top8, im_b, u_b)),
-                )
-                for c in range(2):
-                    for i in range(3):
-                        work[j, b, pl.ds(base + 8 * i, 8), 128 * c : 128 * c + 128] = tiles[c][i]
+            made = []
+            for sp in range(2):
+                for b in range(2):
+                    (re_a, im_a, u_a), (re_b, im_b, u_b) = got[2 * sp][b], got[2 * sp + 1][b]
+                    re_b, im_b = sroll(re_b), sroll(im_b)
+                    tiles = (
+                        (re_a, jnp.where(top8, u_a, re_b), jnp.where(top8, re_b, sroll(u_b))),
+                        (im_a, jnp.where(top8, sroll(u_a), im_b), jnp.where(top8, im_b, u_b)),
+                    )
+                    made += [(24 * sp + 8 * i, b, c, tiles[c][i]) for c in range(2) for i in range(3)]
+            base = pl.multiple_of(h * 48, 8)
+            for at, b, c, tile in made:
+                work[j, b, pl.ds(base + at, 8), 128 * c : 128 * c + 128] = tile
             return 0
 
-        lax.fori_loop(0, owners // 2, unpack, 0)
+        lax.fori_loop(0, owners // 4, unpack, 0, unroll=2)
         for b in range(2):
             v = work[j, b]
             work[j, b] = v + dot3(split(v), (a_hi[...], a_lo[...]), NT)
 
         @pl.when(has_up)
-        def _(j=j):
+        def _():
             pltpu.make_async_remote_copy(
                 src_ref=work.at[j], dst_ref=from_down.at[j], send_sem=su.at[j], recv_sem=rd.at[j],
                 device_id=up_dev, device_id_type=MESH,
             ).start()
 
         @pl.when(has_down)
-        def _(j=j):
+        def _():
             pltpu.make_async_remote_copy(
                 src_ref=work.at[j], dst_ref=from_up.at[j], send_sem=sd.at[j], recv_sem=ru.at[j],
                 device_id=down_dev, device_id_type=MESH,
             ).start()
 
+
+    def finish(j):
         @pl.when(has_up)
-        def _(j=j):
+        def _():
             pltpu.make_async_copy(from_up.at[j], from_up.at[j], ru.at[j]).wait()
 
         @pl.when(has_down)
-        def _(j=j):
+        def _():
             pltpu.make_async_copy(from_down.at[j], from_down.at[j], rd.at[j]).wait()
 
         third = []
@@ -434,33 +475,51 @@
         )
         scratch[...] = v + dot3((r_hi[...], r_lo[...]), split(v), NN)
 
-        def repack(sp, _, j=j):
+        def repack(h, _):
             top8 = sub((8, 128)) < 4
-            base = pl.multiple_of(sp * 24, 8)
-            out = [[], []]
-            for b in range(2):
-                (a0, a1, a2), (i0, i1, i2) = [
-                    [scratch[pl.ds(base + c * count + 8 * i, 8), 128 * b : 128 * b + 128] for i in range(3)]
-                    for c in range(2)
+            base = pl.multiple_of(h * 48, 8)
+            loaded = [
+                [
+                    [
+                        [scratch[pl.ds(base + 24 * sp + c * count + 8 * i, 8), 128 * b : 128 * b + 128] for i in range(3)]
+                        for c in range(2)
+                    ]
+                    for b in range(2)
                 ]
-                r1, r2, q1, q2 = sroll(a1), sroll(a2), sroll(i1), sroll(i2)
-                out[0].append((a0, i0, jnp.where(top8, a1, q1)))
-                out[1].append((jnp.where(top8, r1, r2), jnp.where(top8, q1, q2), jnp.where(top8, r2, i2)))
-            for k in range(2):
-                s = j * owners + 2 * sp + k
-                (re0, im0, u0), (re1, im1, u1) = out[k]
-                t = dense(re0, re1, im0, im1)
-                last, rest = dense_half(u0, u1)
-                for i in range(3):
-                    reply_m[s, 8 * i : 8 * i + 8, :] = t[i]
-                reply_m[s, 24:32, :] = last
-                reply_t[s] = rest
+                for sp in range(2)
+            ]
+            made = []
+            for sp in range(2):
+                out = [[], []]
+                for b in range(2):
+                    (a0, a1, a2), (i0, i1, i2) = loaded[sp][b]
+                    r1, r2, q1, q2 = sroll(a1), sroll(a2), sroll(i1), sroll(i2)
+                    out[0].append((a0, i0, jnp.where(top8, a1, q1)))
+                    out[1].append((jnp.where(top8, r1, r2), jnp.where(top8, q1, q2), jnp.where(top8, r2, i2)))
+                for k in range(2):
+                    (re0, im0, u0), (re1, im1, u1) = out[k]
+                    made.append((*dense(re0, re1, im0, im1), *dense_half(u0, u1)))
+            for k, t in enumerate(made):
+                at = j * owners + 4 * h + k
+                for i in range(4):
+                    reply_m[at, 8 * i : 8 * i + 8, :] = t[i]
+                reply_t[at] = t[4]
             return 0
 
-        lax.fori_loop(0, owners // 2, repack, 0)
+        lax.fori_loop(0, owners // 4, repack, 0, unroll=2)
         send_chunk(
-            j, reply_m, reply_t, back_m, back_t, turned_home, home_of, me_owner, s2m, s2t, r2m, r2t, sa
+            j, (0, owners), reply_m, reply_t, back_m, back_t, turned_home, home_of, me_owner,
+            s2m.at[j], s2t, r2m, r2t, sa,
         )
+
+    advance(0, range(GATES))
+    receive(0)
+    advance(1, range(GATES))
+    receive(1)
+    finish(0)
+    finish(1)
+    receive(2)
+    finish(2)
 
     @pl.when(at_home)
     def _():
@@ -468,7 +527,9 @@
 
     wait_sent(got_w, 0, s1w)
     for j in range(CHUNKS):
-        wait_sent(sent_m, j * owners, s1m.at[j])
+        if j == CHUNKS - 1:
+            for k in range(GATES):
+                gate(j, k)
         wait_sent(sent_t, j * owners, s1t.at[j])
 
         @pl.when(has_up)
@@ -494,38 +555,41 @@
         decay8 = jnp.where(row8 == k, ar[k], decay8)
         decay4 = jnp.where(row8 % 4 == k % 4, ar[8 + k % 4], decay4)
 
-    def group(g, _):
-        points = [jnp.full((8, 128), ab[4 * g + i], f32) for i in range(4)]
-        flat = angle_lanes(points)
-        a, b = 2 * g, 2 * g + 1
-        ta = [main[a, 8 * i : 8 * i + 8, :] for i in range(4)]
-        tb = [main[b, 8 * i : 8 * i + 8, :] for i in range(4)]
+    def group(h, _):
         low = lane((8, 128)) < 64
-        b0, b1, b3 = lroll(tb[0], 64), lroll(tb[1], 64), lroll(tb[3], 64)
-        a1, a2 = lroll(ta[1], 64), lroll(ta[2], 64)
-        re = (ta[0], jnp.where(low, ta[1], b0), jnp.where(low, b0, b1))
-        im = (jnp.where(low, a1, a2), jnp.where(low, a2, tb[1]), tb[2])
-        ra, rb = tail_rows(tail[a]), tail_rows(tail[b])
-        u = (ta[3], jnp.where(low, ra, b3), jnp.where(low, b3, lroll(rb, 64)))
         top = sub((8, 128)) < 4
-        for i in range(3):
-            k = 3 * g + i
-            at = pl.ds(pl.multiple_of(k * 128, 128), 128)
-            co, si = phase(0.5 * pot[0:8, at])
-            d = jnp.exp(-0.5 * (decay8 + flat[i]))
-            co, si = d * co, d * si
-            out[pl.ds(2 * k, 8, stride=2 * blocks), :] = co * re[i] + si * im[i]
-            out[pl.ds(2 * k + 1, 8, stride=2 * blocks), :] = co * im[i] - si * re[i]
-            p4 = pot[8:12, at]
-            co, si = phase(0.5 * jnp.concatenate([p4, p4], axis=0))
-            d = jnp.exp(-0.5 * (decay4 + flat[i]))
-            co, si = d * co, d * si
-            v = co * u[i] + jnp.where(top, si, -si) * sroll(u[i])
+        made = []
+        for g in [2 * h, 2 * h + 1]:
+            flat = angle_lanes([jnp.full((8, 128), ab[4 * g + i], f32) for i in range(4)])
+            a, b = 2 * g, 2 * g + 1
+            ta = [main[a, 8 * i : 8 * i + 8, :] for i in range(4)]
+            tb = [main[b, 8 * i : 8 * i + 8, :] for i in range(4)]
+            b0, b1, b3 = lroll(tb[0], 64), lroll(tb[1], 64), lroll(tb[3], 64)
+            a1, a2 = lroll(ta[1], 64), lroll(ta[2], 64)
+            re = (ta[0], jnp.where(low, ta[1], b0), jnp.where(low, b0, b1))
+            im = (jnp.where(low, a1, a2), jnp.where(low, a2, tb[1]), tb[2])
+            ra, rb = tail_rows(tail[a]), tail_rows(tail[b])
+            u = (ta[3], jnp.where(low, ra, b3), jnp.where(low, b3, lroll(rb, 64)))
+            for i in range(3):
+                k = 3 * g + i
+                at = pl.ds(pl.multiple_of(k * 128, 128), 128)
+                co, si = phase(0.5 * pot[0:8, at])
+                d = jnp.exp(-0.5 * (decay8 + flat[i]))
+                co, si = d * co, d * si
+                p4 = pot[8:12, at]
+                co4, si4 = phase(0.5 * jnp.concatenate([p4, p4], axis=0))
+                d = jnp.exp(-0.5 * (decay4 + flat[i]))
+                co4, si4 = d * co4, d * si4
+                v = co4 * u[i] + jnp.where(top, si4, -si4) * sroll(u[i])
+                made.append((k, co * re[i] + si * im[i], co * im[i] - si * re[i], v))
+        for k, re, im, v in made:
+            out[pl.ds(2 * k, 8, stride=2 * blocks), :] = re
+            out[pl.ds(2 * k + 1, 8, stride=2 * blocks), :] = im
             out[pl.ds(16 * blocks + 2 * k, 4, stride=2 * blocks), :] = v[0:4]
             out[pl.ds(16 * blocks + 2 * k + 1, 4, stride=2 * blocks), :] = v[4:8]
         return 0
 
-    lax.fori_loop(0, groups, group, 0)
+    lax.fori_loop(0, groups // 2, group, 0, unroll=2)
 
 
 def body(wave_in, potential, absorb_radial, absorb_bond, coriolis_weight, ladder, angle_step, bond_step, radial_step):
@@ -550,8 +614,8 @@
         in_specs=[full] * 5,
         out_specs=(full, full),
         scratch_shapes=[
-            VMEM((rows * blocks, 128), f32),
-            VMEM((96 * groups, 128), f32),
+            VMEM((rows * (blocks + 1), 128), f32),
+            VMEM((121 * groups, 128), f32),
             VMEM((8 * groups, 8 * groups), bf16),
             VMEM((8 * groups, 8 * groups), bf16),
         ],
@@ -585,7 +649,7 @@
             VMEM((2 * count, 2 * count), bf16),
             VMEM((2 * count, 256), f32),
             VMEM((1, 2, ANGLES, ANGLES), f32), dma, dma,
-            many, many, dma, many, many, dma,
+            pltpu.SemaphoreType.DMA((CHUNKS, GATES)), many, dma, many, many, dma,
             many, many, many, many,
             many, many, many, many,
         ],

time: 133 us -> 109 us (0.82)
  Pallas kernels: 127 us -> 102 us
    pallas_call x1, Pallas kernels: 102 us -> 90.2 us  [body(): pl.pallas_call(functools.partial(turn_kernel, nz, top), out_shape=(shape(...]
    pallas_call x1, Pallas kernels: 15.6 us -> 7.33 us  [body(): pl.pallas_call(functools.partial(before_kernel, groups), out_shape=(shape...]
    pallas_call x1, Pallas kernels: 9.12 us -> 4.32 us  [body(): pl.pallas_call(functools.partial(after_kernel, groups), out_shape=shape((...]
where the time goes in v1:
time: 109 us; the launch traced here: 107 us
  Pallas kernels  102 us (94%)
  local copies, waits for them, and re-layouts  5.42 us (5%)
    pallas_call x1, Pallas kernels, body(): pl.pallas_call(functools.partial(turn_kernel, nz, top), out_shape=(shape(...  90.2 us
    pallas_call x1, Pallas kernels, body(): pl.pallas_call(functools.partial(before_kernel, groups), out_shape=(shape...  7.33 us
    pallas_call x1, Pallas kernels, body(): pl.pallas_call(functools.partial(after_kernel, groups), out_shape=shape((...  4.32 us
    unnamed x18, local copies, waits for them, and re-layouts  4.1 us

profile of v1, /device:TPU:69, one launch (start us, length us, event | category | flops | bytes accessed | tf_op | source)
XLA Modules:
  0.0 107.3 jit_solution(9673489293516705583)
XLA Ops:
  0.0 0.7 pad_bitcast_fusion.weight
  0.7 0.7 pad_bitcast_fusion.1.ar
  1.3 0.0 copy-start
  1.3 1.3 %copy-done = f32[12,18432]{1,0:T(8,128)S(1)} copy-done((f32[12,18432]{1,0:T(8,128)S(1)}, f32[12,18432]{1,0:T(8,128)}, u32[]{:S(2)}) %copy-start) | copy-done | bytes 884760
  2.6 0.0 copy-start.4
  2.6 1.0 copy-done.4
  3.6 0.0 copy-start.7
  3.6 0.7 copy-done.7
  4.3 0.0 copy-start.3
  4.3 0.0 copy-start.5
  4.3 0.0 copy-start.6
  4.3 7.3 %before.1 = (f32[96,32,128]{2,1,0:T(8,128)S(1)}, f32[96,4,128]{2,1,0:T(4,128)S(1)}) custom-call(f32[3456,128]{1,0:T(8,128)} %bitcast.16, f32[12,18432]{1,0:T(8,128)S(1)} %copy-done, f32[1,128]{1,0:T(1,128)S(1)} %pad_bitcast_fusion.1.ar, f32[1,192]{1,0:T(1,128)S(1)} %bitcast.15, f32[2,192,192]{2,1,0:T(8,128)S(1)} %copy-done.4), custom_call_target="tpu_custom_call" | custom-call | tf_op jit(solution)/shard_map/before/pallas_call | solution.py:611
  11.6 0.0 copy-start.2
  11.6 1.1 %copy-done.2 = f32[96,32,128]{2,1,0:T(8,128)} copy-done((f32[96,32,128]{2,1,0:T(8,128)}, f32[96,32,128]{2,1,0:T(8,128)S(1)}, u32[]{:S(2)}) %copy-start.2) | copy-done | bytes 1572888
  12.8 0.0 copy-start.1
  12.8 0.0 copy-start.8
  12.8 0.0 copy-done.3
  12.8 0.0 copy-done.5
  12.8 0.0 copy-done.6
  12.8 90.2 %turn.1 = (f32[96,32,128]{2,1,0:T(8,128)S(1)}, f32[96,4,128]{2,1,0:T(4,128)S(1)}) custom-call(f32[96,32,128]{2,1,0:T(8,128)} %copy-done.2, f32[96,4,128]{2,1,0:T(4,128)S(1)} %get-tuple-element.10.sent_t, f32[1,128]{1,0:T(1,128)S(1)} %pad_bitcast_fusion.weight, f32[1,2,96,96]{3,2,1,0:T(8,128)S(1)} %copy-done.5, f32[96,96]{1,0:T(8,128)S(1)} %copy-done.6, ...), custom_call_target="tpu_custom_call" | custom-call | tf_op jit(solution)/shard_map/turn/pallas_call | solution.py:626
  103.0 0.0 copy-done.1
  103.0 0.0 copy-done.8
  103.0 4.3 %after.1 = f32[3456,128]{1,0:T(8,128)} custom-call(f32[96,32,128]{2,1,0:T(8,128)S(1)} %get-tuple-element.11.main, f32[96,4,128]{2,1,0:T(4,128)S(1)} %get-tuple-element.12.tail, f32[12,18432]{1,0:T(8,128)S(1)} %copy-done.1, f32[12]{0:T(128)S(1)} %copy-done.8, f32[192]{0:T(256)S(1)} %copy-done.7), custom_call_target="tpu_custom_call" | custom-call | tf_op jit(solution)/shard_map/after/pallas_call | solution.py:659
Async XLA Ops:
  1.3 1.3 %copy-start = (f32[12,18432]{1,0:T(8,128)S(1)}, f32[12,18432]{1,0:T(8,128)}, u32[]{:S(2)}) copy-start(f32[12,18432]{1,0:T(8,128)} %pot.3) | copy-start | bytes 2654212
  2.6 1.0 copy-start.4
  3.6 0.7 copy-start.7
  4.3 8.5 %copy-start.3 = (f32[2,384,384]{2,1,0:T(8,128)S(1)}, f32[2,384,384]{2,1,0:T(8,128)}, u32[]{:S(2)}) copy-start(f32[2,384,384]{2,1,0:T(8,128)} %radial.1) | copy-start | bytes 3538948
  4.3 8.5 %copy-start.5 = (f32[1,2,96,96]{3,2,1,0:T(8,128)S(1)}, f32[1,2,96,96]{3,2,1,0:T(8,128)}, u32[]{:S(2)}) copy-start(f32[1,2,96,96]{3,2,1,0:T(8,128)} %angle.1) | copy-start | bytes 221188
  4.3 8.5 %copy-start.6 = (f32[96,96]{1,0:T(8,128)S(1)}, f32[96,96]{1,0:T(8,128)}, u32[]{:S(2)}) copy-start(f32[96,96]{1,0:T(8,128)} %ladder.1) | copy-start | bytes 110596
  11.6 1.1 %copy-start.2 = (f32[96,32,128]{2,1,0:T(8,128)}, f32[96,32,128]{2,1,0:T(8,128)S(1)}, u32[]{:S(2)}) copy-start(f32[96,32,128]{2,1,0:T(8,128)S(1)} %get-tuple-element.9.sent_m) | copy-start | bytes 4718596
  12.8 90.3 %copy-start.1 = (f32[12,18432]{1,0:T(8,128)S(1)}, f32[12,18432]{1,0:T(8,128)}, u32[]{:S(2)}) copy-start(f32[12,18432]{1,0:T(8,128)} %pot.3) | copy-start | bytes 2654212
  12.8 90.3 %copy-start.8 = (f32[12]{0:T(128)S(1)}, f32[12]{0:T(128)}, u32[]{:S(2)}) copy-start(f32[12]{0:T(128)} %ar.1) | copy-start | bytes 148

commit v2 on v1

--- a/solution.py
+++ b/solution.py
@@ -101,33 +101,111 @@
     return jnp.where(n < 96, a, b), jnp.where(n < 64, b, c), jnp.where(n < 32, c, d)
 
 
-def before_kernel(groups, wave, pot, ar, ab, bond, main, tail, pots, bigw, mat_hi, mat_lo):
+def step_kernel(
+    groups, nz, top,
+    wave_h, pot_h, ar_h, ab_h, weight_h, angle_h, ladder_h, bond_h, radial_h, out_h,
+    wave, pot, ar, ab, weight, angle, ladder, bond, radial,
+    pots, bigw, mat, xf, xh, xl, damps, factors, sent_m, sent_t,
+    got_m, got_t, got_w, own_w, wide, work, from_up, from_down, reply_m, reply_t, back_m, back_t, outv,
+    a_hi, a_lo, u_hi, u_lo, d_hi, d_lo, r_hi, r_lo, scratch,
+    angles, in_sems, wave_sems, out_sems, sa_sem, ra_sem,
+    s1m, s1t, s1w, r1m, r1t, r1w, su, sd, ru, rd, s2m, s2t, r2m, r2t,
+):
     bonds = 4 * groups
     blocks = 3 * groups
     pitch = blocks + 1
-
-    def turn(k, _):
-        at = pl.ds(pl.multiple_of(k * 128, 128), 128)
-        pots[pl.ds(k, 8, stride=pitch), :] = pot[0:8, at]
-        pots[pl.ds(8 * pitch + k, 4, stride=pitch), :] = pot[8:12, at]
+    per_row = 2 * blocks
+    owners = 4 * nz
+    ka, sa = lax.axis_index("ka"), lax.axis_index("sa")
+    x, yh = ka // 2, ka % 2
+    yl, z, core = sa // (2 * nz), (sa // 2) % nz, sa % 2
+    y = 2 * yh + yl
+    helicity = 2 * x + core
+    me_owner = y * nz + z
+    at_home = core == yh
+
+    def owner_of(q, c):
+        oy, oz = q // nz, q % nz
+        return (2 * x + oy // 2, (oy % 2) * (2 * nz) + oz * 2 + c)
+
+    def home_of(s):
+        return (2 * x + core, s)
+
+    def turned(i):
+        return ((y + i % 4) % 4) * nz + (z + nz // 2 + i // 4) % nz
+
+    def turned_home(i):
+        c, iy, iz = i % 2, (i // 2) % 2, i // 4
+        return ((yl + iy) % 2) * (2 * nz) + ((z + nz // 2 + iz) % nz) * 2 + c
+
+    has_up, has_down = helicity < top, helicity > 0
+    kx_up = jnp.where(core == 0, x, x + 1)
+    kx_down = jnp.where(core == 1, x, x - 1)
+    up_dev = (2 * kx_up + yh, yl * (2 * nz) + z * 2 + 1 - core)
+    down_dev = (2 * kx_down + yh, yl * (2 * nz) + z * 2 + 1 - core)
+
+    names = ((bond_h, bond), (ab_h, ab), (ar_h, ar), (pot_h, pot), (angle_h, angle), (weight_h, weight))
+    names = names + ((ladder_h, ladder), (radial_h, radial))
+    loads = [pltpu.make_async_copy(a, b, in_sems.at[k]) for k, (a, b) in enumerate(names)]
+    wave_loads = [
+        pltpu.make_async_copy(
+            wave_h.at[pl.ds(2 * h * per_row, 2 * per_row)], wave.at[pl.ds(2 * h * per_row, 2 * per_row)], wave_sems.at[h]
+        )
+        for h in range(ROWS // 2)
+    ]
+    for load in loads[:4] + wave_loads + loads[4:]:
+        load.start()
+
+    barrier = pltpu.get_barrier_semaphore()
+
+    def greet(i, _):
+        q, s = turned(i), turned_home(i)
+
+        @pl.when(jnp.logical_not(at_home & (q == me_owner)))
+        def _():
+            pl.semaphore_signal(barrier, inc=1, device_id=owner_of(q, yh), device_id_type=MESH)
+
+        @pl.when(jnp.logical_not(at_home & (s == sa)))
+        def _():
+            pl.semaphore_signal(barrier, inc=1, device_id=home_of(s), device_id_type=MESH)
+
         return 0
 
-    lax.fori_loop(0, blocks, turn, 0, unroll=4)
+    lax.fori_loop(0, owners, greet, 0)
+
+    @pl.when(has_up)
+    def _():
+        pl.semaphore_signal(barrier, inc=1, device_id=up_dev, device_id_type=MESH)
+
+    @pl.when(has_down)
+    def _():
+        pl.semaphore_signal(barrier, inc=1, device_id=down_dev, device_id_type=MESH)
+
+    for load in loads[:3]:
+        load.wait()
 
     place = lax.broadcasted_iota(jnp.int32, (bonds, bonds), 1)
     point = lax.broadcasted_iota(jnp.int32, (bonds, bonds), 0)
+    third_groups = groups // CHUNKS
+    wide_rows = 4 * third_groups
     perm = jnp.where(point == 4 * (place % groups) + place // groups, 1.0, 0.0).astype(bf16)
+    inside = place % wide_rows
+    point_of = 4 * (third_groups * (place // wide_rows) + inside % third_groups) + inside // third_groups
+    row_perm = jnp.where(point == point_of, 1.0, 0.0).astype(bf16)
     for c in range(2):
-        for part, mat in zip(split(bond[c]), (mat_hi, mat_lo)):
+        for k, part in enumerate(split(bond[c])):
             cols = jnp.dot(part, perm, preferred_element_type=f32).astype(bf16)
-            rows = lax.dot_general(perm, cols, (((0,), (0,)), ((), ())), preferred_element_type=f32)
+            rows = lax.dot_general(row_perm, cols, (((0,), (0,)), ((), ())), preferred_element_type=f32)
             rows = rows.astype(bf16)
-            if c == 0:
-                mat[0:bonds, 0:bonds] = rows
-                mat[bonds:, bonds:] = rows
-            else:
-                mat[0:bonds, bonds:] = -rows
-                mat[bonds:, 0:bonds] = rows
+            for j in range(CHUNKS):
+                own = rows[j * wide_rows : (j + 1) * wide_rows]
+                at = 2 * k * wide_rows
+                if c == 0:
+                    mat[j, at : at + wide_rows, 0:bonds] = own
+                    mat[j, at + wide_rows : at + 2 * wide_rows, bonds:] = own
+                else:
+                    mat[j, at : at + wide_rows, bonds:] = -own
+                    mat[j, at + wide_rows : at + 2 * wide_rows, 0:bonds] = own
 
     grid = (groups, bonds)
     cols = []
@@ -135,13 +213,25 @@
         mine = jnp.where(lane(grid) == 4 * sub(grid) + i, jnp.broadcast_to(ab[...], grid), 0.0)
         cols.append(jnp.exp(-0.5 * jnp.sum(mine, axis=1, keepdims=True)))
     damp = angle_lanes([jnp.broadcast_to(c, (groups, 128)) for c in cols])
+    for i in range(3):
+        damps[i] = damp[i]
     decay = jnp.exp(-0.5 * ar[...])
 
-    def two_rows(h, _):
+    loads[3].wait()
+
+    def turn(k, _):
+        at = pl.ds(pl.multiple_of(k * 128, 128), 128)
+        pots[pl.ds(k, 8, stride=pitch), :] = pot[0:8, at]
+        pots[pl.ds(8 * pitch + k, 4, stride=pitch), :] = pot[8:12, at]
+        return 0
+
+    lax.fori_loop(0, blocks, turn, 0, unroll=4)
+
+    def two_rows(h):
         sides = []
         for k in range(2):
             r = 2 * h + k
-            own = jnp.sum(jnp.where(lane((1, 128)) == r, decay, 0.0), axis=1, keepdims=True)
+            own = jnp.sum(jnp.where(lane((1, ROWS)) == r, decay, 0.0), axis=1, keepdims=True)
             re, im = [], []
             for i in range(3):
                 x = wave[pl.ds(r * 2 * blocks + 2 * i, groups, stride=6), :]
@@ -153,17 +243,31 @@
                 im.append(co * y - si * x)
             sides.append(jnp.concatenate(spread(*re) + spread(*im), axis=0))
         x = jnp.concatenate(sides, axis=1)
-        x = x + dot3((mat_hi[...], mat_lo[...]), split(x), NN)
-        for k in range(2):
-            r = 2 * h + k
-            for c in range(2):
-                row = jnp.where(r < 8, r + 8 * c, r + 8 + 4 * c)
-                for i in range(4):
-                    at = (4 * c + i) * groups
-                    bigw[pl.ds(i + 5 * row, groups, stride=121), :] = x[at : at + groups, 128 * k : 128 * k + 128]
-        return 0
-
-    lax.fori_loop(0, ROWS // 2, two_rows, 0, unroll=True)
+        xf[h] = x
+        xh[h], xl[h] = split(x)
+
+    def bond_step(j):
+        for h in range(ROWS // 2):
+            o = jnp.dot(mat[j], xh[h], preferred_element_type=f32)
+            o = o[0 : 2 * wide_rows] + (
+                o[2 * wide_rows :] + jnp.dot(mat[j, 0 : 2 * wide_rows], xl[h], preferred_element_type=f32)
+            )
+            for k in range(2):
+                r = 2 * h + k
+                for c in range(2):
+                    row = r + 8 * c if r < 8 else r + 8 + 4 * c
+                    for i in range(4):
+                        at = (4 * c + i) * third_groups
+                        base = (4 * c + i) * groups + j * third_groups
+                        v = o[at : at + third_groups, 128 * k : 128 * k + 128]
+                        v = v + xf[h, base : base + third_groups, 128 * k : 128 * k + 128]
+                        bigw[pl.ds(i + 5 * row + 121 * j * third_groups, third_groups, stride=121), :] = v
+
+    for h in range(ROWS // 2):
+        wave_loads[h].wait()
+    for h in range(ROWS // 2):
+        two_rows(h)
+    bond_step(0)
 
     def pack(h, _):
         pairs = [PACK * h + k for k in range(PACK)]
@@ -176,74 +280,12 @@
         ]
         for p, t in zip(pairs, made):
             for k in range(4):
-                main[p, 8 * k : 8 * k + 8, :] = t[k]
-            tail[p] = t[4]
+                sent_m[p, 8 * k : 8 * k + 8, :] = t[k]
+            sent_t[p] = t[4]
         return 0
 
-    lax.fori_loop(0, bonds // 2 // PACK, pack, 0, unroll=2)
-
-
-def turn_kernel(
-    nz, top, sent_m, sent_t, weight, angle, ladder, radial, back_m, back_t,
-    got_m, got_t, got_w, own_w, wide, work, from_up, from_down, reply_m, reply_t,
-    a_hi, a_lo, u_hi, u_lo, d_hi, d_lo, r_hi, r_lo, scratch,
-    angles, sa_sem, ra_sem, s1m, s1t, s1w, r1m, r1t, r1w, su, sd, ru, rd, s2m, s2t, r2m, r2t,
-):
-    owners = 4 * nz
-    ka, sa = lax.axis_index("ka"), lax.axis_index("sa")
-    x, yh = ka // 2, ka % 2
-    yl, z, core = sa // (2 * nz), (sa // 2) % nz, sa % 2
-    y = 2 * yh + yl
-    helicity = 2 * x + core
-    me_owner = y * nz + z
-    at_home = core == yh
-
-    def owner_of(q, c):
-        oy, oz = q // nz, q % nz
-        return (2 * x + oy // 2, (oy % 2) * (2 * nz) + oz * 2 + c)
-
-    def home_of(s):
-        return (2 * x + core, s)
-
-    def turned(i):
-        return ((y + i % 4) % 4) * nz + (z + nz // 2 + i // 4) % nz
-
-    def turned_home(i):
-        c, iy, iz = i % 2, (i // 2) % 2, i // 4
-        return ((yl + iy) % 2) * (2 * nz) + ((z + nz // 2 + iz) % nz) * 2 + c
-
-    has_up, has_down = helicity < top, helicity > 0
-    kx_up = jnp.where(core == 0, x, x + 1)
-    kx_down = jnp.where(core == 1, x, x - 1)
-    up_dev = (2 * kx_up + yh, yl * (2 * nz) + z * 2 + 1 - core)
-    down_dev = (2 * kx_down + yh, yl * (2 * nz) + z * 2 + 1 - core)
-
-    barrier = pltpu.get_barrier_semaphore()
-
-    def greet(i, _):
-        q, s = turned(i), turned_home(i)
-
-        @pl.when(jnp.logical_not(at_home & (q == me_owner)))
-        def _():
-            pl.semaphore_signal(barrier, inc=1, device_id=owner_of(q, yh), device_id_type=MESH)
-
-        @pl.when(jnp.logical_not(at_home & (s == sa)))
-        def _():
-            pl.semaphore_signal(barrier, inc=1, device_id=home_of(s), device_id_type=MESH)
-
-        return 0
-
-    lax.fori_loop(0, owners, greet, 0)
-
-    @pl.when(has_up)
-    def _():
-        pl.semaphore_signal(barrier, inc=1, device_id=up_dev, device_id_type=MESH)
-
-    @pl.when(has_down)
-    def _():
-        pl.semaphore_signal(barrier, inc=1, device_id=down_dev, device_id_type=MESH)
-
-    own_w[...] = weight[...]
+    batches = owners // PACK
+    lax.fori_loop(0, batches, pack, 0, unroll=2)
 
     expected = 2 * owners - 2 * at_home.astype(jnp.int32)
     expected = expected + has_up.astype(jnp.int32) + has_down.astype(jnp.int32)
@@ -304,17 +346,6 @@
         def _():
             wait_bytes(ref, owners, start, sem)
 
-    to_other = pltpu.make_async_remote_copy(
-        src_ref=angle, dst_ref=angles, send_sem=sa_sem, recv_sem=ra_sem,
-        device_id=(2 * x + 1 - yh, sa), device_id_type=MESH,
-    )
-
-    @pl.when(at_home)
-    def _():
-        to_other.start()
-        angles[...] = angle[...]
-
-    lax.fori_loop(0, owners, send_weight, 0)
     size = owners // GATES
     mine_at = (nz // 2) * 4 // size
 
@@ -346,6 +377,27 @@
 
     for k in range(GATES):
         first_send(0, k)
+
+    loads[4].wait()
+    loads[5].wait()
+    own_w[...] = jnp.zeros((1, 128), f32)
+    own_w[:, 0:ROWS] = weight[...]
+    to_other = pltpu.make_async_remote_copy(
+        src_ref=angle, dst_ref=angles, send_sem=sa_sem, recv_sem=ra_sem,
+        device_id=(2 * x + 1 - yh, sa), device_id_type=MESH,
+    )
+
+    @pl.when(at_home)
+    def _():
+        to_other.start()
+        angles[...] = angle[...]
+
+    lax.fori_loop(0, owners, send_weight, 0)
+    for j in range(1, CHUNKS):
+        bond_step(j)
+        lax.fori_loop(j * batches, (j + 1) * batches, pack, 0, unroll=2)
+    loads[6].wait()
+    loads[7].wait()
 
     def fill(parts, hi, lo, shape):
         scratch[0 : shape[0], 0 : shape[1]] = jnp.zeros(shape, f32)
@@ -379,6 +431,33 @@
         @pl.when(jnp.logical_not(has))
         def _(buf=buf):
             buf[...] = jnp.zeros(buf.shape, f32)
+
+    def column(row_of):
+        shape = (8, ROWS)
+        mine = jnp.where(lane(shape) == row_of(sub(shape)), jnp.broadcast_to(decay, shape), 0.0)
+        return jnp.sum(mine, axis=1, keepdims=True)
+
+    decay8, decay4 = column(lambda n: n), column(lambda n: 8 + n % 4)
+
+    def make_factor(g, _):
+        top4 = sub((8, 128)) < 4
+        made = []
+        for i in range(3):
+            at = pl.ds(pl.multiple_of((3 * g + i) * 128, 128), 128)
+            flat = damps[i, pl.ds(g, 1), :]
+            p4 = pot[8:12, at]
+            for half, own in ((pot[0:8, at], decay8), (jnp.concatenate([p4, p4], axis=0), decay4)):
+                co, si = phase(0.5 * half)
+                d = own * flat
+                made.append((at, d * co, d * si))
+        for n, (at, co, si) in enumerate(made):
+            if n % 2:
+                si = jnp.where(top4, si, -si)
+            factors[2 * (n % 2), :, at] = co
+            factors[2 * (n % 2) + 1, :, at] = si
+        return 0
+
+    lax.fori_loop(0, groups, make_factor, 0, unroll=2)
 
     @pl.when(jnp.logical_not(at_home))
     def _():
@@ -512,6 +591,47 @@
             s2m.at[j], s2t, r2m, r2t, sa,
         )
 
+    def leave(j):
+        wait_bytes(back_m, owners, j * owners, r2m.at[j])
+        wait_bytes(back_t, owners, j * owners, r2t.at[j])
+
+        def group(h, _):
+            low = lane((8, 128)) < 64
+            made = []
+            for g in [2 * h, 2 * h + 1]:
+                a, b = 2 * g, 2 * g + 1
+                ta = [back_m[a, 8 * i : 8 * i + 8, :] for i in range(4)]
+                tb = [back_m[b, 8 * i : 8 * i + 8, :] for i in range(4)]
+                b0, b1, b3 = lroll(tb[0], 64), lroll(tb[1], 64), lroll(tb[3], 64)
+                a1, a2 = lroll(ta[1], 64), lroll(ta[2], 64)
+                re = (ta[0], jnp.where(low, ta[1], b0), jnp.where(low, b0, b1))
+                im = (jnp.where(low, a1, a2), jnp.where(low, a2, tb[1]), tb[2])
+                ra, rb = tail_rows(back_t[a]), tail_rows(back_t[b])
+                u = (ta[3], jnp.where(low, ra, b3), jnp.where(low, b3, lroll(rb, 64)))
+                for i in range(3):
+                    k = 3 * g + i
+                    at = pl.ds(pl.multiple_of(k * 128, 128), 128)
+                    co, si, co4, si4 = [factors[n, :, at] for n in range(4)]
+                    v = co4 * u[i] + si4 * sroll(u[i])
+                    made.append((k, co * re[i] + si * im[i], co * im[i] - si * re[i], v))
+            for k, re, im, v in made:
+                outv[pl.ds(2 * k, 8, stride=per_row), :] = re
+                outv[pl.ds(2 * k + 1, 8, stride=per_row), :] = im
+                outv[pl.ds(8 * per_row + 2 * k, 4, stride=per_row), :] = v[0:4]
+                outv[pl.ds(8 * per_row + 2 * k + 1, 4, stride=per_row), :] = v[4:8]
+            return 0
+
+        part = groups // CHUNKS // 2
+        lax.fori_loop(j * part, (j + 1) * part, group, 0, unroll=2)
+        width = per_row // CHUNKS
+
+        def store(r, _):
+            at = pl.ds(pl.multiple_of(r * per_row + j * width, 8), width)
+            pltpu.make_async_copy(outv.at[at], out_h.at[at], out_sems.at[j]).start()
+            return 0
+
+        lax.fori_loop(0, ROWS, store, 0)
+
     advance(0, range(GATES))
     receive(0)
     advance(1, range(GATES))
@@ -520,6 +640,8 @@
     finish(1)
     receive(2)
     finish(2)
+    for j in range(CHUNKS):
+        leave(j)
 
     @pl.when(at_home)
     def _():
@@ -541,94 +663,51 @@
             pltpu.make_async_copy(work.at[j], work.at[j], sd.at[j]).wait()
 
     for j in range(CHUNKS):
-        wait_bytes(back_m, owners, j * owners, r2m.at[j])
-        wait_bytes(back_t, owners, j * owners, r2t.at[j])
         wait_sent(reply_m, j * owners, s2m.at[j])
         wait_sent(reply_t, j * owners, s2t.at[j])
-
-
-def after_kernel(groups, main, tail, pot, ar, ab, out):
-    blocks = 3 * groups
-    row8 = sub((8, 1))
-    decay8, decay4 = jnp.zeros((8, 1), f32), jnp.zeros((8, 1), f32)
-    for k in range(8):
-        decay8 = jnp.where(row8 == k, ar[k], decay8)
-        decay4 = jnp.where(row8 % 4 == k % 4, ar[8 + k % 4], decay4)
-
-    def group(h, _):
-        low = lane((8, 128)) < 64
-        top = sub((8, 128)) < 4
-        made = []
-        for g in [2 * h, 2 * h + 1]:
-            flat = angle_lanes([jnp.full((8, 128), ab[4 * g + i], f32) for i in range(4)])
-            a, b = 2 * g, 2 * g + 1
-            ta = [main[a, 8 * i : 8 * i + 8, :] for i in range(4)]
-            tb = [main[b, 8 * i : 8 * i + 8, :] for i in range(4)]
-            b0, b1, b3 = lroll(tb[0], 64), lroll(tb[1], 64), lroll(tb[3], 64)
-            a1, a2 = lroll(ta[1], 64), lroll(ta[2], 64)
-            re = (ta[0], jnp.where(low, ta[1], b0), jnp.where(low, b0, b1))
-            im = (jnp.where(low, a1, a2), jnp.where(low, a2, tb[1]), tb[2])
-            ra, rb = tail_rows(tail[a]), tail_rows(tail[b])
-            u = (ta[3], jnp.where(low, ra, b3), jnp.where(low, b3, lroll(rb, 64)))
-            for i in range(3):
-                k = 3 * g + i
-                at = pl.ds(pl.multiple_of(k * 128, 128), 128)
-                co, si = phase(0.5 * pot[0:8, at])
-                d = jnp.exp(-0.5 * (decay8 + flat[i]))
-                co, si = d * co, d * si
-                p4 = pot[8:12, at]
-                co4, si4 = phase(0.5 * jnp.concatenate([p4, p4], axis=0))
-                d = jnp.exp(-0.5 * (decay4 + flat[i]))
-                co4, si4 = d * co4, d * si4
-                v = co4 * u[i] + jnp.where(top, si4, -si4) * sroll(u[i])
-                made.append((k, co * re[i] + si * im[i], co * im[i] - si * re[i], v))
-        for k, re, im, v in made:
-            out[pl.ds(2 * k, 8, stride=2 * blocks), :] = re
-            out[pl.ds(2 * k + 1, 8, stride=2 * blocks), :] = im
-            out[pl.ds(16 * blocks + 2 * k, 4, stride=2 * blocks), :] = v[0:4]
-            out[pl.ds(16 * blocks + 2 * k + 1, 4, stride=2 * blocks), :] = v[4:8]
-        return 0
-
-    lax.fori_loop(0, groups // 2, group, 0, unroll=2)
+        whole = pl.ds(0, ROWS * per_row // CHUNKS)
+        pltpu.make_async_copy(outv.at[whole], out_h.at[whole], out_sems.at[j]).wait()
 
 
 def body(wave_in, potential, absorb_radial, absorb_bond, coriolis_weight, ladder, angle_step, bond_step, radial_step):
     rows, columns = wave_in.shape[2:]
     blocks = columns // 128
     groups = blocks // 3
+    bonds = 4 * groups
     nz = lax.axis_size("sa") // 4
     owners = 4 * nz
     top = lax.axis_size("ka") - 1
     count = radial_step.shape[1]
-    full = pl.BlockSpec(memory_space=VMEM)
-    smem = pl.BlockSpec(memory_space=pltpu.SMEM)
     hbm = pl.BlockSpec(memory_space=pl.ANY)
-    shape = jax.ShapeDtypeStruct
     wave = wave_in.reshape(2, rows, blocks, 128).transpose(1, 2, 0, 3).reshape(rows * blocks * 2, 128)
-    pad = jnp.pad(absorb_radial, (0, 128 - rows)).reshape(1, 128)
-    weight = jnp.pad(coriolis_weight, (0, 128 - rows)).reshape(1, 128)
     messages = CHUNKS * owners
-    main, tail = pl.pallas_call(
-        functools.partial(before_kernel, groups),
-        out_shape=(shape((messages, 32, 128), f32), shape((messages, 4, 128), f32)),
-        in_specs=[full] * 5,
-        out_specs=(full, full),
+    dma, many = pltpu.SemaphoreType.DMA, pltpu.SemaphoreType.DMA((CHUNKS,))
+    small = VMEM((256, 256), bf16)
+    out = pl.pallas_call(
+        functools.partial(step_kernel, groups, nz, top),
+        out_shape=jax.ShapeDtypeStruct((rows * blocks * 2, 128), f32),
+        in_specs=[hbm] * 9,
+        out_specs=hbm,
         scratch_shapes=[
+            VMEM((rows * blocks * 2, 128), f32),
+            VMEM((rows, columns), f32),
+            VMEM((1, rows), f32),
+            VMEM((1, bonds), f32),
+            VMEM((1, rows), f32),
+            VMEM((1, 2, ANGLES, ANGLES), f32),
+            VMEM((ANGLES, ANGLES), f32),
+            VMEM((2, bonds, bonds), f32),
+            VMEM((2, count, count), f32),
             VMEM((rows * (blocks + 1), 128), f32),
             VMEM((121 * groups, 128), f32),
-            VMEM((8 * groups, 8 * groups), bf16),
-            VMEM((8 * groups, 8 * groups), bf16),
-        ],
-        compiler_params=pltpu.CompilerParams(vmem_limit_bytes=50 << 20),
-        name="before",
-    )(wave, potential, pad, absorb_bond.reshape(1, -1), bond_step)
-    dma, many = pltpu.SemaphoreType.DMA, pltpu.SemaphoreType.DMA((CHUNKS,))
-    back_m, back_t = pl.pallas_call(
-        functools.partial(turn_kernel, nz, top),
-        out_shape=(shape((messages, 32, 128), f32), shape((messages, 4, 128), f32)),
-        in_specs=[hbm, hbm, full, full, full, full],
-        out_specs=(hbm, hbm),
-        scratch_shapes=[
+            VMEM((CHUNKS, 4 * bonds // CHUNKS, 2 * bonds), bf16),
+            VMEM((rows // 2, 2 * bonds, 256), f32),
+            VMEM((rows // 2, 2 * bonds, 256), bf16),
+            VMEM((rows // 2, 2 * bonds, 256), bf16),
+            VMEM((3, groups, 128), f32),
+            VMEM((4, 8, columns), f32),
+            VMEM((messages, 32, 128), f32),
+            VMEM((messages, 4, 128), f32),
             VMEM((messages, 32, 128), f32),
             VMEM((messages, 4, 128), f32),
             VMEM((owners, 1, 128), f32),
@@ -639,31 +718,25 @@
             VMEM((CHUNKS, 2, count, 256), f32),
             VMEM((messages, 32, 128), f32),
             VMEM((messages, 4, 128), f32),
-            VMEM((256, 256), bf16),
-            VMEM((256, 256), bf16),
-            VMEM((256, 256), bf16),
-            VMEM((256, 256), bf16),
-            VMEM((256, 256), bf16),
-            VMEM((256, 256), bf16),
+            VMEM((messages, 32, 128), f32),
+            VMEM((messages, 4, 128), f32),
+            VMEM((rows * blocks * 2, 128), f32),
+            small, small, small, small, small, small,
             VMEM((2 * count, 2 * count), bf16),
             VMEM((2 * count, 2 * count), bf16),
             VMEM((2 * count, 256), f32),
-            VMEM((1, 2, ANGLES, ANGLES), f32), dma, dma,
+            VMEM((1, 2, ANGLES, ANGLES), f32),
+            pltpu.SemaphoreType.DMA((8,)), pltpu.SemaphoreType.DMA((rows // 2,)), many, dma, dma,
             pltpu.SemaphoreType.DMA((CHUNKS, GATES)), many, dma, many, many, dma,
             many, many, many, many,
             many, many, many, many,
         ],
-        compiler_params=pltpu.CompilerParams(collective_id=0, has_side_effects=True, vmem_limit_bytes=50 << 20),
-        name="turn",
-    )(main, tail, weight, angle_step, ladder, radial_step)
-    out = pl.pallas_call(
-        functools.partial(after_kernel, groups),
-        out_shape=shape((rows * blocks * 2, 128), f32),
-        in_specs=[full, full, full, smem, smem],
-        out_specs=full,
-        compiler_params=pltpu.CompilerParams(vmem_limit_bytes=50 << 20),
-        name="after",
-    )(back_m, back_t, potential, absorb_radial, absorb_bond)
+        compiler_params=pltpu.CompilerParams(collective_id=0, has_side_effects=True, vmem_limit_bytes=58 << 20),
+        name="step",
+    )(
+        wave, potential, absorb_radial.reshape(1, -1), absorb_bond.reshape(1, -1), coriolis_weight.reshape(1, -1),
+        angle_step, ladder, bond_step, radial_step,
+    )
     return out.reshape(rows, blocks, 2, 128).transpose(2, 0, 1, 3).reshape(1, 2, rows, columns)
 
 

time: 109 us -> 101 us (0.927)
  Pallas kernels: 102 us -> 96.7 us
  local copies, waits for them, and re-layouts: 5.42 us -> 2.8 us
    pallas_call x3 -> x1, Pallas kernels: 102 us -> 96.7 us  [body(): pl.pallas_call(functools.partial(step_kernel, groups, nz, top), out_shape...]
    reshape x2 -> x0, local copies, waits for them, and re-layouts: 1.31 us -> none  [the longest x1 0.66 us: body(): weight = jnp.pad(coriolis_weight, (0, 128 - rows)).reshape(1, 128)]
    unnamed x18 -> x1, local copies, waits for them, and re-layouts: 4.1 us -> 2.8 us
where the time goes in v2:
time: 101 us; the launch traced here: 99.5 us
  Pallas kernels  96.7 us (96%)
  local copies, waits for them, and re-layouts  2.8 us (3%)
    pallas_call x1, Pallas kernels, body(): pl.pallas_call(functools.partial(step_kernel, groups, nz, top), out_shape...  96.7 us
    unnamed x1, local copies, waits for them, and re-layouts  2.8 us

profile of v2, /device:TPU:69, one launch (start us, length us, event | category | flops | bytes accessed | tf_op | source)
XLA Modules:
  0.0 99.5 jit_solution(3159352259950161272)
XLA Ops:
  0.0 96.7 %step.1 = f32[3456,128]{1,0:T(8,128)} custom-call(f32[3456,128]{1,0:T(8,128)} %bitcast.14, f32[12,18432]{1,0:T(8,128)} %pot_h.1, f32[1,12]{1,0:T(1,128)} %bitcast.16, f32[1,192]{1,0:T(1,128)} %bitcast.15, f32[1,12]{1,0:T(1,128)} %bitcast.17, f32[1,2,96,96]{3,2,1,0:T(8,128)} %angle_h.1, f32[96,96]{1,0:T(8,128)} %ladder_h.1, f32[2,192,192]{2,1,0:T(8,128)} %bond_h.1, ...), custom_call_target="tpu_custom_call" | custom-call | tf_op jit(solution)/shard_map/step/pallas_call | solution.py:686
  96.7 2.8 %copy.13 = f32[1,2,12,18432]{3,1,2,0:T(2,128)} copy(f32[1,2,12,18432]{3,1,2,0:T(2,128)} %bitcast.13) | data formatting | bytes 3538944

commit v3 on v2

--- a/solution.py
+++ b/solution.py
@@ -16,6 +16,7 @@
 ANGLES = 96
 PACK = 4
 GATES = 4
+ORDER = (2, 1, 3, 0)
 f32, bf16 = jnp.float32, jnp.bfloat16
 
 
@@ -138,6 +139,12 @@
         c, iy, iz = i % 2, (i // 2) % 2, i // 4
         return ((yl + iy) % 2) * (2 * nz) + ((z + nz // 2 + iz) % nz) * 2 + c
 
+    def early_home(i):
+        c, iy, iz = i % 2, (i // 2) % 2, i // 4
+        first = 3
+        away = jnp.where(iz < first, iz, first + (z + nz // 2 + iz) % (nz - first))
+        return ((yl + iy) % 2) * (2 * nz) + away * 2 + c
+
     has_up, has_down = helicity < top, helicity > 0
     kx_up = jnp.where(core == 0, x, x + 1)
     kx_down = jnp.where(core == 1, x, x - 1)
@@ -153,7 +160,7 @@
         )
         for h in range(ROWS // 2)
     ]
-    for load in loads[:4] + wave_loads + loads[4:]:
+    for load in loads[:4] + wave_loads:
         load.start()
 
     barrier = pltpu.get_barrier_semaphore()
@@ -265,6 +272,8 @@
 
     for h in range(ROWS // 2):
         wave_loads[h].wait()
+    for load in loads[4:]:
+        load.start()
     for h in range(ROWS // 2):
         two_rows(h)
     bond_step(0)
@@ -368,8 +377,8 @@
             def _():
                 wait_bytes(sent_m, size, 0, s1m.at[j, k])
 
-    def advance(j, parts):
-        for k in parts:
+    def advance(j):
+        for k in ORDER:
             if j < CHUNKS:
                 gate(j, k)
             if j + 1 < CHUNKS:
@@ -586,8 +595,10 @@
             return 0
 
         lax.fori_loop(0, owners // 4, repack, 0, unroll=2)
+
+    def reply(j, k):
         send_chunk(
-            j, (0, owners), reply_m, reply_t, back_m, back_t, turned_home, home_of, me_owner,
+            j, (k * size, k * size + size), reply_m, reply_t, back_m, back_t, early_home, home_of, me_owner,
             s2m.at[j], s2t, r2m, r2t, sa,
         )
 
@@ -632,14 +643,21 @@
 
         lax.fori_loop(0, ROWS, store, 0)
 
-    advance(0, range(GATES))
+    advance(0)
     receive(0)
-    advance(1, range(GATES))
+    advance(1)
     receive(1)
     finish(0)
+    for k in ORDER:
+        gate(2, k)
+        reply(0, k)
+    receive(2)
     finish(1)
-    receive(2)
+    for k in range(GATES):
+        reply(1, k)
     finish(2)
+    for k in range(GATES):
+        reply(2, k)
     for j in range(CHUNKS):
         leave(j)
 
@@ -649,9 +667,6 @@
 
     wait_sent(got_w, 0, s1w)
     for j in range(CHUNKS):
-        if j == CHUNKS - 1:
-            for k in range(GATES):
-                gate(j, k)
         wait_sent(sent_t, j * owners, s1t.at[j])
 
         @pl.when(has_up)

time: 101 us -> 99.9 us (0.989); the launches traced: 99.5 us -> 99.8 us
  no operation moved by 1% of the time
where the time goes in v3:
time: 99.9 us; the launch traced here: 99.8 us
  Pallas kernels  97 us (97%)
  local copies, waits for them, and re-layouts  2.8 us (3%)
    pallas_call x1, Pallas kernels, body(): pl.pallas_call(functools.partial(step_kernel, groups, nz, top), out_shape...  97 us
    unnamed x1, local copies, waits for them, and re-layouts  2.8 us

profile of v3, /device:TPU:69, one launch (start us, length us, event | category | flops | bytes accessed | tf_op | source)
XLA Modules:
  0.0 99.8 jit_solution(18013573198883481190)
XLA Ops:
  0.0 97.0 %step.1 = f32[3456,128]{1,0:T(8,128)} custom-call(f32[3456,128]{1,0:T(8,128)} %bitcast.14, f32[12,18432]{1,0:T(8,128)} %pot_h.1, f32[1,12]{1,0:T(1,128)} %bitcast.16, f32[1,192]{1,0:T(1,128)} %bitcast.15, f32[1,12]{1,0:T(1,128)} %bitcast.17, f32[1,2,96,96]{3,2,1,0:T(8,128)} %angle_h.1, f32[96,96]{1,0:T(8,128)} %ladder_h.1, f32[2,192,192]{2,1,0:T(8,128)} %bond_h.1, ...), custom_call_target="tpu_custom_call" | custom-call | tf_op jit(solution)/shard_map/step/pallas_call | solution.py:701
  97.0 2.8 %copy.13 = f32[1,2,12,18432]{3,1,2,0:T(2,128)} copy(f32[1,2,12,18432]{3,1,2,0:T(2,128)} %bitcast.13) | data formatting | bytes 3538944

commit v4 on v3

--- a/solution.py
+++ b/solution.py
@@ -278,8 +278,7 @@
         two_rows(h)
     bond_step(0)
 
-    def pack(h, _):
-        pairs = [PACK * h + k for k in range(PACK)]
+    def pack_all(pairs):
         loaded = [
             [bigw[pl.ds(121 * (p // 2) + 2 * (p % 2) + b + 40 * k, 8, stride=5), :] for b in range(2) for k in range(3)]
             for p in pairs
@@ -291,10 +290,12 @@
             for k in range(4):
                 sent_m[p, 8 * k : 8 * k + 8, :] = t[k]
             sent_t[p] = t[4]
+
+    def pack(h, _):
+        pack_all([PACK * h + k for k in range(PACK)])
         return 0
 
     batches = owners // PACK
-    lax.fori_loop(0, batches, pack, 0, unroll=2)
 
     expected = 2 * owners - 2 * at_home.astype(jnp.int32)
     expected = expected + has_up.astype(jnp.int32) + has_down.astype(jnp.int32)
@@ -385,6 +386,9 @@
                 first_send(j + 1, k)
 
     for k in range(GATES):
+        for i in range(nz // GATES):
+            plane = (z + nz // 2 + k * (nz // GATES) + i) % nz
+            pack_all([iy * nz + plane for iy in range(4)])
         first_send(0, k)
 
     loads[4].wait()
@@ -598,7 +602,7 @@
 
     def reply(j, k):
         send_chunk(
-            j, (k * size, k * size + size), reply_m, reply_t, back_m, back_t, early_home, home_of, me_owner,
+            j, (k * size, k * size + size), reply_m, reply_t, back_m, back_t, turned_home if j == 0 else early_home, home_of, me_owner,
             s2m.at[j], s2t, r2m, r2t, sa,
         )
 

time: 99.9 us -> 99.7 us (level)
  no operation moved by 1% of the time
where the time goes in v4:
time: 99.7 us; the launch traced here: 99.6 us
  Pallas kernels  96.8 us (97%)
  local copies, waits for them, and re-layouts  2.8 us (3%)
    pallas_call x1, Pallas kernels, body(): pl.pallas_call(functools.partial(step_kernel, groups, nz, top), out_shape...  96.8 us
    unnamed x1, local copies, waits for them, and re-layouts  2.8 us

profile of v4, /device:TPU:69, one launch (start us, length us, event | category | flops | bytes accessed | tf_op | source)
XLA Modules:
  0.0 99.6 jit_solution(11207445344161336499)
XLA Ops:
  0.0 96.8 %step.1 = f32[3456,128]{1,0:T(8,128)} custom-call(f32[3456,128]{1,0:T(8,128)} %bitcast.14, f32[12,18432]{1,0:T(8,128)} %pot_h.1, f32[1,12]{1,0:T(1,128)} %bitcast.16, f32[1,192]{1,0:T(1,128)} %bitcast.15, f32[1,12]{1,0:T(1,128)} %bitcast.17, f32[1,2,96,96]{3,2,1,0:T(8,128)} %angle_h.1, f32[96,96]{1,0:T(8,128)} %ladder_h.1, f32[2,192,192]{2,1,0:T(8,128)} %bond_h.1, ...), custom_call_target="tpu_custom_call" | custom-call | tf_op jit(solution)/shard_map/step/pallas_call | solution.py:705
  96.8 2.8 %copy.13 = f32[1,2,12,18432]{3,1,2,0:T(2,128)} copy(f32[1,2,12,18432]{3,1,2,0:T(2,128)} %bitcast.13) | data formatting | bytes 3538944
